TPU v7x, 32 devices: a whole 2x2x4 slice. The times are simulated.
32 devices in a mesh: node: 2 (over y), space: 16 (over z, x, core).
Axes of the slice: x: 2, y: 2, z: 4, core: 2. Of those that a mesh axis runs over, the one named last changes fastest.
Arguments:
- grain_ids: int32 [64, 16, 128], P('space'), may hold values from 0 to 7
- peak_heat: float32 [64, 16, 128], P('space'), may hold values from 0.5 to 1
Outputs:
- node_states: float32 [2, 8, 64, 16, 128], P('node', None, 'space')
All inputs are finite; a program needn't handle non-finite values.
Results may differ from a plain program's by a relative error of at most 0.0001.
Values sent between devices are 32-bit elements; how exact they have to be, the bound alone decides.
A program may use at most 64 MiB of HBM per device.

v0:
```python
import math

import jax
import jax.numpy as jnp
import numpy as np
from jax import lax
from jax.sharding import PartitionSpec as P

P_SIZE = 8
NODE_DEV = 1
SWEEPS = 3
JACOBI = 2
STEPS = 2


time_step = 0.25
cross_coef = 1.5
base_heat = 0.45
activation = 3.0


def with_halo(block, sides, width):
    for axis, dim in sides:
        count = lax.axis_size(axis)
        forward = [(i, i + 1) for i in range(count - 1)]
        forward.append((count - 1, 0))
        backward = [(target, source) for source, target in forward]
        low = lax.ppermute(
            lax.slice_in_dim(block, block.shape[dim] - width, None, axis=dim), axis, forward
        )
        high = lax.ppermute(lax.slice_in_dim(block, 0, width, axis=dim), axis, backward)
        block = jnp.concatenate([low, block, high], axis=dim)
    return block


def broadcast(block, axis, source):
    block = jnp.where(lax.axis_index(axis) == source, block, jnp.zeros_like(block))
    return lax.psum(block, axis)


def legendre_pair(count, point):
    before = 1.0
    current = point
    for degree in range(2, count + 1):
        following = ((2 * degree - 1) * point * current - (degree - 1) * before) / degree
        before = current
        current = following
    return (current, before)


def radau_value(count, point):
    high, low = legendre_pair(count, point)
    high_prev, low_prev = legendre_pair(count - 1, point)
    value = high - low
    slope_high = count * (point * high - low) / (point * point - 1.0)
    slope_low = (count - 1) * (point * high_prev - low_prev) / (point * point - 1.0)
    return (value, slope_high - slope_low)


def radau_table(count):
    roots = [1.0]
    for index in range(1, count):
        point = math.cos(2.0 * math.pi * index / (2 * count - 1))
        for repeat in range(100):
            value, slope = radau_value(count, point)
            point = point - value / slope
        roots.append(point)
    roots = sorted(roots)
    times_list = [(value + 1.0) / 2.0 for value in roots]
    times_list[-1] = 1.0
    table = []
    for row_index in range(count):
        upper = times_list[row_index]
        row_values = []
        for column in range(count):
            poly = [1.0]
            for other in range(count):
                if other != column:
                    scale = times_list[column] - times_list[other]
                    shifted = [0.0] + poly
                    scaled = [c * times_list[other] for c in poly] + [0.0]
                    poly = [(shifted[i] - scaled[i]) / scale for i in range(len(shifted))]
            integral_value = 0.0
            for power in range(len(poly)):
                integral_value += poly[power] * upper ** (power + 1) / (power + 1)
            row_values.append(integral_value)
        table.append(row_values)
    return (np.array(times_list), np.array(table))


def drive(field):
    squares = field * field
    total = jnp.sum(squares, axis=-4, keepdims=True)
    return -field + squares * field + 2.0 * cross_coef * field * (total - squares)


def near_sum(extended):
    inner = extended[..., 1:-1, :, :]
    result = extended[..., 2:, :, :] + extended[..., :-2, :, :]
    result = result + jnp.roll(inner, -1, -2) + jnp.roll(inner, 1, -2)
    return result + jnp.roll(inner, -1, -1) + jnp.roll(inner, 1, -1)


def heat_mobility(peak, moment):
    middle = 0.5 * time_step * STEPS
    theta = base_heat + (peak - base_heat) * jnp.exp(-(((moment - middle) / middle) ** 2))
    return jnp.exp(activation * (1.0 - 1.0 / theta))


def rate_on(extended, mobility):
    inner = extended[..., 1:-1, :, :]
    return -mobility * (drive(inner) - (near_sum(extended) - 6.0 * inner))


def relax_on(extended, goal, factor):
    inner = extended[..., 1:-1, :, :]
    return (goal + factor * (near_sum(extended) - drive(inner))) / (1.0 + 6.0 * factor)


def on_device(grain_ids, peak_heat):
    total_nodes = lax.axis_size("node") * NODE_DEV
    node_times, table = radau_table(total_nodes)
    weights = jnp.asarray(table, jnp.float32)
    first = lax.axis_index("node") * NODE_DEV
    times = lax.dynamic_slice_in_dim(jnp.asarray(node_times, jnp.float32), first, NODE_DEV, 0)
    my_rows = lax.dynamic_slice_in_dim(weights, first, NODE_DEV, 0)
    taus = times.reshape((NODE_DEV, 1, 1, 1, 1))
    orders = jnp.arange(P_SIZE, dtype=jnp.int32)
    start = (grain_ids[None] == orders[:, None, None, None]).astype(jnp.float32)
    states = None
    for step_index in range(STEPS):
        moments = (step_index + times) * time_step
        mobility = heat_mobility(peak_heat[None], moments[:, None, None, None])[:, None]
        factor = time_step * taus * mobility
        start_wide = with_halo(start, (("space", 1),), 1)
        rates = rate_on(start_wide[None], mobility)
        states = jnp.broadcast_to(start[None], rates.shape)
        for sweep_index in range(SWEEPS):
            piece = lax.all_gather(rates, "node", axis=0, tiled=True)
            coefs = lax.slice_in_dim(my_rows, 0, piece.shape[0], axis=1)
            quad = jnp.zeros_like(rates) + jnp.tensordot(
                coefs, piece, axes=1, precision=lax.Precision.HIGHEST
            )
            goal = start[None] + time_step * quad - time_step * taus * rates
            last = sweep_index + 1 == SWEEPS
            passes = JACOBI if last else JACOBI + 1
            for relax_index in range(passes):
                extended = with_halo(states, (("space", 2),), 1)
                if relax_index < JACOBI:
                    states = relax_on(extended, goal, factor)
                else:
                    rates = rate_on(extended, mobility)
        if step_index + 1 < STEPS:
            start = broadcast(states[-1], "node", lax.axis_size("node") - 1)
    return states


def solution(mesh):
    in_specs = (P("space", None, None), P("space", None, None))
    out_specs = P("node", None, "space", None, None)
    return jax.shard_map(
        on_device, mesh=mesh, in_specs=in_specs, out_specs=out_specs, check_vma=False
    )
```

profile of v0, /device:TPU:0, one launch (start us, length us, event | category | flops | bytes accessed | tf_op | source)
XLA Modules:
  0.0 197.2 jit_solution(5471797001832641271)
XLA Ops:
  7.3 5.5 %collective-permute-start.2 = (f32[1,8,1,16,128]{4,3,2,1,0:T(8,128)S(1)}, f32[1,8,1,16,128]{4,3,2,1,0:T(8,128)S(1)}, u32[]{:S(2)}, u32[]{:S(2)}) collective-permute-start(f32[1,8,1,16,128]{4,3,2,1,0:T(8,128)S(1)} %get-tuple-element.167), channel_id=1, source_target_pairs={{1,0},{2,1},{3,2},{4,3},{5,4},{6,5},{7,6},{8,7},{9,8},{10,9},{11,1... | collective-permute-start | bytes 196616 | tf_op jit(solution)/shard_map/ppermute | solution.py:31
  12.9 4.5 %collective-permute-start.1 = (f32[8,1,16,128]{3,2,1,0:T(8,128)S(1)}, f32[8,1,16,128]{3,2,1,0:T(8,128)S(1)}, u32[]{:S(2)}, u32[]{:S(2)}) collective-permute-start(f32[8,1,16,128]{3,2,1,0:T(8,128)S(1)} %get-tuple-element.166), channel_id=1, source_target_pairs={{1,0},{2,1},{3,2},{4,3},{5,4},{6,5},{7,6},{8,7},{9,8},{10,9},{11,1... | collective-permute-start | bytes 196616 | tf_op jit(solution)/shard_map/ppermute | solution.py:31
  21.1 7.0 %all_gather.18 = f32[2,8,4,16,128]{4,3,2,1,0:T(8,128)S(1)} all-gather(f32[1,8,4,16,128]{4,3,2,1,0:T(8,128)S(1)} %fusion.21), channel_id=1, replica_groups=mesh['node'=2,'space'=16] {'node'}, dimensions={0}, use_global_device_ids=true | all-gather | bytes 786432 | tf_op jit(solution)/shard_map/all_gather | solution.py:139
  30.9 2.6 %collective-permute-start.4 = (f32[1,8,1,16,128]{4,3,2,1,0:T(8,128)S(1)}, f32[1,8,1,16,128]{4,3,2,1,0:T(8,128)S(1)}, u32[]{:S(2)}, u32[]{:S(2)}) collective-permute-start(f32[1,8,1,16,128]{4,3,2,1,0:T(8,128)S(1)} %get-tuple-element.155), channel_id=1, source_target_pairs={{1,0},{2,1},{3,2},{4,3},{5,4},{6,5},{7,6},{8,7},{9,8},{10,9},{11,1... | collective-permute-start | bytes 196616 | tf_op jit(solution)/shard_map/ppermute | solution.py:31
  35.5 4.6 %collective-permute-done.5 = f32[1,8,1,16,128]{4,3,2,1,0:T(8,128)S(1)} collective-permute-done((f32[1,8,1,16,128]{4,3,2,1,0:T(8,128)S(1)}, f32[1,8,1,16,128]{4,3,2,1,0:T(8,128)S(1)}, u32[]{:S(2)}, u32[]{:S(2)}) %collective-permute-start.5) | collective-permute-done | bytes 65568 | tf_op jit(solution)/shard_map/ppermute | solution.py:28
  42.8 4.5 %collective-permute-done.7 = f32[1,8,1,16,128]{4,3,2,1,0:T(8,128)S(1)} collective-permute-done((f32[1,8,1,16,128]{4,3,2,1,0:T(8,128)S(1)}, f32[1,8,1,16,128]{4,3,2,1,0:T(8,128)S(1)}, u32[]{:S(2)}, u32[]{:S(2)}) %collective-permute-start.7) | collective-permute-done | bytes 65568 | tf_op jit(solution)/shard_map/ppermute | solution.py:28
  47.6 7.0 %all_gather.19 = f32[2,8,4,16,128]{4,3,2,1,0:T(8,128)S(1)} all-gather(f32[1,8,4,16,128]{4,3,2,1,0:T(8,128)S(1)} %get-tuple-element.29), channel_id=1, replica_groups=mesh['node'=2,'space'=16] {'node'}, dimensions={0}, use_global_device_ids=true | all-gather | bytes 786432 | tf_op jit(solution)/shard_map/all_gather | solution.py:139
  59.2 4.5 %collective-permute-done.9 = f32[1,8,1,16,128]{4,3,2,1,0:T(8,128)S(1)} collective-permute-done((f32[1,8,1,16,128]{4,3,2,1,0:T(8,128)S(1)}, f32[1,8,1,16,128]{4,3,2,1,0:T(8,128)S(1)}, u32[]{:S(2)}, u32[]{:S(2)}) %collective-permute-start.9) | collective-permute-done | bytes 65568 | tf_op jit(solution)/shard_map/ppermute | solution.py:28
  66.4 4.5 %collective-permute-done.11 = f32[1,8,1,16,128]{4,3,2,1,0:T(8,128)S(1)} collective-permute-done((f32[1,8,1,16,128]{4,3,2,1,0:T(8,128)S(1)}, f32[1,8,1,16,128]{4,3,2,1,0:T(8,128)S(1)}, u32[]{:S(2)}, u32[]{:S(2)}) %collective-permute-start.11) | collective-permute-done | bytes 65568 | tf_op jit(solution)/shard_map/ppermute | solution.py:28
  71.2 7.2 %all_gather.20 = f32[2,8,4,16,128]{4,3,2,1,0:T(8,128)S(1)} all-gather(f32[1,8,4,16,128]{4,3,2,1,0:T(8,128)S(1)} %get-tuple-element.23), channel_id=1, replica_groups=mesh['node'=2,'space'=16] {'node'}, dimensions={0}, use_global_device_ids=true | all-gather | bytes 786432 | tf_op jit(solution)/shard_map/all_gather | solution.py:139
  83.0 4.5 %collective-permute-done.13 = f32[1,8,1,16,128]{4,3,2,1,0:T(8,128)S(1)} collective-permute-done((f32[1,8,1,16,128]{4,3,2,1,0:T(8,128)S(1)}, f32[1,8,1,16,128]{4,3,2,1,0:T(8,128)S(1)}, u32[]{:S(2)}, u32[]{:S(2)}) %collective-permute-start.13) | collective-permute-done | bytes 65568 | tf_op jit(solution)/shard_map/ppermute | solution.py:28
  88.7 20.6 %all-reduce.2.cloned.1.call-done = f32[8,4,16,128]{3,2,1,0:T(8,128)} async-done(((f32[8,4,16,128]{3,2,1,0:T(8,128)}), f32[8,4,16,128]{3,2,1,0:T(8,128)}) %all-reduce.2.cloned.1.call-update) | async-done | bytes 262160 | tf_op jit(solution)/shard_map/psum | solution.py:38
  111.5 3.3 %collective-permute-start.16 = (f32[1,8,1,16,128]{4,3,2,1,0:T(8,128)S(1)}, f32[1,8,1,16,128]{4,3,2,1,0:T(8,128)S(1)}, u32[]{:S(2)}, u32[]{:S(2)}) collective-permute-start(f32[1,8,1,16,128]{4,3,2,1,0:T(8,128)S(1)} %get-tuple-element.105), channel_id=1, source_target_pairs={{1,0},{2,1},{3,2},{4,3},{5,4},{6,5},{7,6},{8,7},{9,8},{10,9},{11,1... | collective-permute-start | bytes 196616 | tf_op jit(solution)/shard_map/ppermute | solution.py:31
  114.9 4.5 %collective-permute-start.15 = (f32[8,1,16,128]{3,2,1,0:T(8,128)S(1)}, f32[8,1,16,128]{3,2,1,0:T(8,128)S(1)}, u32[]{:S(2)}, u32[]{:S(2)}) collective-permute-start(f32[8,1,16,128]{3,2,1,0:T(8,128)S(1)} %get-tuple-element.104), channel_id=1, source_target_pairs={{1,0},{2,1},{3,2},{4,3},{5,4},{6,5},{7,6},{8,7},{9,8},{10,9},{11,1... | collective-permute-start | bytes 196616 | tf_op jit(solution)/shard_map/ppermute | solution.py:31
  119.4 2.5 %collective-permute-done.14 = f32[8,1,16,128]{3,2,1,0:T(8,128)S(1)} collective-permute-done((f32[8,1,16,128]{3,2,1,0:T(8,128)S(1)}, f32[8,1,16,128]{3,2,1,0:T(8,128)S(1)}, u32[]{:S(2)}, u32[]{:S(2)}) %collective-permute-start.14) | collective-permute-done | bytes 65568 | tf_op jit(solution)/shard_map/ppermute | solution.py:28
  122.6 7.0 %all_gather.21 = f32[2,8,4,16,128]{4,3,2,1,0:T(8,128)S(1)} all-gather(f32[1,8,4,16,128]{4,3,2,1,0:T(8,128)S(1)} %fusion.53), channel_id=1, replica_groups=mesh['node'=2,'space'=16] {'node'}, dimensions={0}, use_global_device_ids=true | all-gather | bytes 786432 | tf_op jit(solution)/shard_map/all_gather | solution.py:139
  132.5 2.8 %collective-permute-start.18 = (f32[1,8,1,16,128]{4,3,2,1,0:T(8,128)S(1)}, f32[1,8,1,16,128]{4,3,2,1,0:T(8,128)S(1)}, u32[]{:S(2)}, u32[]{:S(2)}) collective-permute-start(f32[1,8,1,16,128]{4,3,2,1,0:T(8,128)S(1)} %get-tuple-element.93), channel_id=1, source_target_pairs={{1,0},{2,1},{3,2},{4,3},{5,4},{6,5},{7,6},{8,7},{9,8},{10,9},{11,1... | collective-permute-start | bytes 196616 | tf_op jit(solution)/shard_map/ppermute | solution.py:31
  137.1 4.6 %collective-permute-done.19 = f32[1,8,1,16,128]{4,3,2,1,0:T(8,128)S(1)} collective-permute-done((f32[1,8,1,16,128]{4,3,2,1,0:T(8,128)S(1)}, f32[1,8,1,16,128]{4,3,2,1,0:T(8,128)S(1)}, u32[]{:S(2)}, u32[]{:S(2)}) %collective-permute-start.19) | collective-permute-done | bytes 65568 | tf_op jit(solution)/shard_map/ppermute | solution.py:28
  144.4 4.5 %collective-permute-done.21 = f32[1,8,1,16,128]{4,3,2,1,0:T(8,128)S(1)} collective-permute-done((f32[1,8,1,16,128]{4,3,2,1,0:T(8,128)S(1)}, f32[1,8,1,16,128]{4,3,2,1,0:T(8,128)S(1)}, u32[]{:S(2)}, u32[]{:S(2)}) %collective-permute-start.21) | collective-permute-done | bytes 65568 | tf_op jit(solution)/shard_map/ppermute | solution.py:28
  149.3 7.0 %all_gather.22 = f32[2,8,4,16,128]{4,3,2,1,0:T(8,128)S(1)} all-gather(f32[1,8,4,16,128]{4,3,2,1,0:T(8,128)S(1)} %get-tuple-element.13), channel_id=1, replica_groups=mesh['node'=2,'space'=16] {'node'}, dimensions={0}, use_global_device_ids=true | all-gather | bytes 786432 | tf_op jit(solution)/shard_map/all_gather | solution.py:139
  160.8 4.8 %collective-permute-done.23 = f32[1,8,1,16,128]{4,3,2,1,0:T(8,128)S(1)} collective-permute-done((f32[1,8,1,16,128]{4,3,2,1,0:T(8,128)S(1)}, f32[1,8,1,16,128]{4,3,2,1,0:T(8,128)S(1)}, u32[]{:S(2)}, u32[]{:S(2)}) %collective-permute-start.23) | collective-permute-done | bytes 65568 | tf_op jit(solution)/shard_map/ppermute | solution.py:28
  168.3 4.5 %collective-permute-done.25 = f32[1,8,1,16,128]{4,3,2,1,0:T(8,128)S(1)} collective-permute-done((f32[1,8,1,16,128]{4,3,2,1,0:T(8,128)S(1)}, f32[1,8,1,16,128]{4,3,2,1,0:T(8,128)S(1)}, u32[]{:S(2)}, u32[]{:S(2)}) %collective-permute-start.25) | collective-permute-done | bytes 65568 | tf_op jit(solution)/shard_map/ppermute | solution.py:28
  173.2 7.0 %all_gather.23 = f32[2,8,4,16,128]{4,3,2,1,0:T(8,128)S(1)} all-gather(f32[1,8,4,16,128]{4,3,2,1,0:T(8,128)S(1)} %get-tuple-element.7), channel_id=1, replica_groups=mesh['node'=2,'space'=16] {'node'}, dimensions={0}, use_global_device_ids=true | all-gather | bytes 786432 | tf_op jit(solution)/shard_map/all_gather | solution.py:139
  184.7 4.5 %collective-permute-done.27 = f32[1,8,1,16,128]{4,3,2,1,0:T(8,128)S(1)} collective-permute-done((f32[1,8,1,16,128]{4,3,2,1,0:T(8,128)S(1)}, f32[1,8,1,16,128]{4,3,2,1,0:T(8,128)S(1)}, u32[]{:S(2)}, u32[]{:S(2)}) %collective-permute-start.27) | collective-permute-done | bytes 65568 | tf_op jit(solution)/shard_map/ppermute | solution.py:28
  (155 shorter events, 47.1 us)
Async XLA Ops:
  6.5 102.7 %all-reduce.2.cloned.1.call-start = ((), (), s32[]{:S(2)}) async-start(), calls=%async_computation | async-start | bytes 524288 | tf_op jit(solution)/shard_map/psum | solution.py:38
  7.3 22.9 %collective-permute-start.2 = (f32[1,8,1,16,128]{4,3,2,1,0:T(8,128)S(1)}, f32[1,8,1,16,128]{4,3,2,1,0:T(8,128)S(1)}, u32[]{:S(2)}, u32[]{:S(2)}) collective-permute-start(f32[1,8,1,16,128]{4,3,2,1,0:T(8,128)S(1)} %get-tuple-element.167), channel_id=1, source_target_pairs={{1,0},{2,1},{3,2},{4,3},{5,4},{6,5},{7,6},{8,7},{9,8},{10,9},{11,1... | collective-permute-start | bytes 196616 | tf_op jit(solution)/shard_map/ppermute | solution.py:31
  12.8 17.4 %collective-permute-start.3 = (f32[1,8,1,16,128]{4,3,2,1,0:T(8,128)S(1)}, f32[1,8,1,16,128]{4,3,2,1,0:T(8,128)S(1)}, u32[]{:S(2)}, u32[]{:S(2)}) collective-permute-start(f32[1,8,1,16,128]{4,3,2,1,0:T(8,128)S(1)} %get-tuple-element.168), channel_id=1, source_target_pairs={{0,1},{1,2},{2,3},{3,4},{4,5},{5,6},{6,7},{7,8},{8,9},{9,10},{10,1... | collective-permute-start | bytes 196616 | tf_op jit(solution)/shard_map/ppermute | solution.py:28
  12.9 7.5 %collective-permute-start = (f32[8,1,16,128]{3,2,1,0:T(8,128)S(1)}, f32[8,1,16,128]{3,2,1,0:T(8,128)S(1)}, u32[]{:S(2)}, u32[]{:S(2)}) collective-permute-start(f32[8,1,16,128]{3,2,1,0:T(8,128)S(1)} %get-tuple-element.165), channel_id=1, source_target_pairs={{0,1},{1,2},{2,3},{3,4},{4,5},{5,6},{6,7},{7,8},{8,9},{9,10},{10,1... | collective-permute-start | bytes 196616 | tf_op jit(solution)/shard_map/ppermute | solution.py:28
  12.9 7.4 %collective-permute-start.1 = (f32[8,1,16,128]{3,2,1,0:T(8,128)S(1)}, f32[8,1,16,128]{3,2,1,0:T(8,128)S(1)}, u32[]{:S(2)}, u32[]{:S(2)}) collective-permute-start(f32[8,1,16,128]{3,2,1,0:T(8,128)S(1)} %get-tuple-element.166), channel_id=1, source_target_pairs={{1,0},{2,1},{3,2},{4,3},{5,4},{6,5},{7,6},{8,7},{9,8},{10,9},{11,1... | collective-permute-start | bytes 196616 | tf_op jit(solution)/shard_map/ppermute | solution.py:31
  30.9 4.5 %collective-permute-start.4 = (f32[1,8,1,16,128]{4,3,2,1,0:T(8,128)S(1)}, f32[1,8,1,16,128]{4,3,2,1,0:T(8,128)S(1)}, u32[]{:S(2)}, u32[]{:S(2)}) collective-permute-start(f32[1,8,1,16,128]{4,3,2,1,0:T(8,128)S(1)} %get-tuple-element.155), channel_id=1, source_target_pairs={{1,0},{2,1},{3,2},{4,3},{5,4},{6,5},{7,6},{8,7},{9,8},{10,9},{11,1... | collective-permute-start | bytes 196616 | tf_op jit(solution)/shard_map/ppermute | solution.py:31
  33.6 6.5 %collective-permute-start.5 = (f32[1,8,1,16,128]{4,3,2,1,0:T(8,128)S(1)}, f32[1,8,1,16,128]{4,3,2,1,0:T(8,128)S(1)}, u32[]{:S(2)}, u32[]{:S(2)}) collective-permute-start(f32[1,8,1,16,128]{4,3,2,1,0:T(8,128)S(1)} %get-tuple-element.156), channel_id=1, source_target_pairs={{0,1},{1,2},{2,3},{3,4},{4,5},{5,6},{6,7},{7,8},{8,9},{9,10},{10,1... | collective-permute-start | bytes 196616 | tf_op jit(solution)/shard_map/ppermute | solution.py:28
  40.9 6.4 %collective-permute-start.7 = (f32[1,8,1,16,128]{4,3,2,1,0:T(8,128)S(1)}, f32[1,8,1,16,128]{4,3,2,1,0:T(8,128)S(1)}, u32[]{:S(2)}, u32[]{:S(2)}) collective-permute-start(f32[1,8,1,16,128]{4,3,2,1,0:T(8,128)S(1)} %get-tuple-element.146), channel_id=1, source_target_pairs={{0,1},{1,2},{2,3},{3,4},{4,5},{5,6},{6,7},{7,8},{8,9},{9,10},{10,1... | collective-permute-start | bytes 196616 | tf_op jit(solution)/shard_map/ppermute | solution.py:28
  57.3 6.4 %collective-permute-start.9 = (f32[1,8,1,16,128]{4,3,2,1,0:T(8,128)S(1)}, f32[1,8,1,16,128]{4,3,2,1,0:T(8,128)S(1)}, u32[]{:S(2)}, u32[]{:S(2)}) collective-permute-start(f32[1,8,1,16,128]{4,3,2,1,0:T(8,128)S(1)} %get-tuple-element.136), channel_id=1, source_target_pairs={{0,1},{1,2},{2,3},{3,4},{4,5},{5,6},{6,7},{7,8},{8,9},{9,10},{10,1... | collective-permute-start | bytes 196616 | tf_op jit(solution)/shard_map/ppermute | solution.py:28
  64.4 2.0 collective-permute-start.10
  64.5 6.4 %collective-permute-start.11 = (f32[1,8,1,16,128]{4,3,2,1,0:T(8,128)S(1)}, f32[1,8,1,16,128]{4,3,2,1,0:T(8,128)S(1)}, u32[]{:S(2)}, u32[]{:S(2)}) collective-permute-start(f32[1,8,1,16,128]{4,3,2,1,0:T(8,128)S(1)} %get-tuple-element.126), channel_id=1, source_target_pairs={{0,1},{1,2},{2,3},{3,4},{4,5},{5,6},{6,7},{7,8},{8,9},{9,10},{10,1... | collective-permute-start | bytes 196616 | tf_op jit(solution)/shard_map/ppermute | solution.py:28
  81.1 6.4 %collective-permute-start.13 = (f32[1,8,1,16,128]{4,3,2,1,0:T(8,128)S(1)}, f32[1,8,1,16,128]{4,3,2,1,0:T(8,128)S(1)}, u32[]{:S(2)}, u32[]{:S(2)}) collective-permute-start(f32[1,8,1,16,128]{4,3,2,1,0:T(8,128)S(1)} %get-tuple-element.116), channel_id=1, source_target_pairs={{0,1},{1,2},{2,3},{3,4},{4,5},{5,6},{6,7},{7,8},{8,9},{9,10},{10,1... | collective-permute-start | bytes 196616 | tf_op jit(solution)/shard_map/ppermute | solution.py:28
  111.5 20.2 %collective-permute-start.16 = (f32[1,8,1,16,128]{4,3,2,1,0:T(8,128)S(1)}, f32[1,8,1,16,128]{4,3,2,1,0:T(8,128)S(1)}, u32[]{:S(2)}, u32[]{:S(2)}) collective-permute-start(f32[1,8,1,16,128]{4,3,2,1,0:T(8,128)S(1)} %get-tuple-element.105), channel_id=1, source_target_pairs={{1,0},{2,1},{3,2},{4,3},{5,4},{6,5},{7,6},{8,7},{9,8},{10,9},{11,1... | collective-permute-start | bytes 196616 | tf_op jit(solution)/shard_map/ppermute | solution.py:31
  114.8 16.9 %collective-permute-start.17 = (f32[1,8,1,16,128]{4,3,2,1,0:T(8,128)S(1)}, f32[1,8,1,16,128]{4,3,2,1,0:T(8,128)S(1)}, u32[]{:S(2)}, u32[]{:S(2)}) collective-permute-start(f32[1,8,1,16,128]{4,3,2,1,0:T(8,128)S(1)} %get-tuple-element.106), channel_id=1, source_target_pairs={{0,1},{1,2},{2,3},{3,4},{4,5},{5,6},{6,7},{7,8},{8,9},{9,10},{10,1... | collective-permute-start | bytes 196616 | tf_op jit(solution)/shard_map/ppermute | solution.py:28
  114.8 7.1 %collective-permute-start.14 = (f32[8,1,16,128]{3,2,1,0:T(8,128)S(1)}, f32[8,1,16,128]{3,2,1,0:T(8,128)S(1)}, u32[]{:S(2)}, u32[]{:S(2)}) collective-permute-start(f32[8,1,16,128]{3,2,1,0:T(8,128)S(1)} %get-tuple-element.103), channel_id=1, source_target_pairs={{0,1},{1,2},{2,3},{3,4},{4,5},{5,6},{6,7},{7,8},{8,9},{9,10},{10,1... | collective-permute-start | bytes 196616 | tf_op jit(solution)/shard_map/ppermute | solution.py:28
  114.9 7.0 %collective-permute-start.15 = (f32[8,1,16,128]{3,2,1,0:T(8,128)S(1)}, f32[8,1,16,128]{3,2,1,0:T(8,128)S(1)}, u32[]{:S(2)}, u32[]{:S(2)}) collective-permute-start(f32[8,1,16,128]{3,2,1,0:T(8,128)S(1)} %get-tuple-element.104), channel_id=1, source_target_pairs={{1,0},{2,1},{3,2},{4,3},{5,4},{6,5},{7,6},{8,7},{9,8},{10,9},{11,1... | collective-permute-start | bytes 196616 | tf_op jit(solution)/shard_map/ppermute | solution.py:31
  132.5 4.7 %collective-permute-start.18 = (f32[1,8,1,16,128]{4,3,2,1,0:T(8,128)S(1)}, f32[1,8,1,16,128]{4,3,2,1,0:T(8,128)S(1)}, u32[]{:S(2)}, u32[]{:S(2)}) collective-permute-start(f32[1,8,1,16,128]{4,3,2,1,0:T(8,128)S(1)} %get-tuple-element.93), channel_id=1, source_target_pairs={{1,0},{2,1},{3,2},{4,3},{5,4},{6,5},{7,6},{8,7},{9,8},{10,9},{11,1... | collective-permute-start | bytes 196616 | tf_op jit(solution)/shard_map/ppermute | solution.py:31
  135.2 6.5 %collective-permute-start.19 = (f32[1,8,1,16,128]{4,3,2,1,0:T(8,128)S(1)}, f32[1,8,1,16,128]{4,3,2,1,0:T(8,128)S(1)}, u32[]{:S(2)}, u32[]{:S(2)}) collective-permute-start(f32[1,8,1,16,128]{4,3,2,1,0:T(8,128)S(1)} %get-tuple-element.94), channel_id=1, source_target_pairs={{0,1},{1,2},{2,3},{3,4},{4,5},{5,6},{6,7},{7,8},{8,9},{9,10},{10,1... | collective-permute-start | bytes 196616 | tf_op jit(solution)/shard_map/ppermute | solution.py:28
  142.5 2.0 collective-permute-start.20
  142.5 6.4 %collective-permute-start.21 = (f32[1,8,1,16,128]{4,3,2,1,0:T(8,128)S(1)}, f32[1,8,1,16,128]{4,3,2,1,0:T(8,128)S(1)}, u32[]{:S(2)}, u32[]{:S(2)}) collective-permute-start(f32[1,8,1,16,128]{4,3,2,1,0:T(8,128)S(1)} %get-tuple-element.84), channel_id=1, source_target_pairs={{0,1},{1,2},{2,3},{3,4},{4,5},{5,6},{6,7},{7,8},{8,9},{9,10},{10,1... | collective-permute-start | bytes 196616 | tf_op jit(solution)/shard_map/ppermute | solution.py:28
  158.9 2.0 collective-permute-start.22
  158.9 6.7 %collective-permute-start.23 = (f32[1,8,1,16,128]{4,3,2,1,0:T(8,128)S(1)}, f32[1,8,1,16,128]{4,3,2,1,0:T(8,128)S(1)}, u32[]{:S(2)}, u32[]{:S(2)}) collective-permute-start(f32[1,8,1,16,128]{4,3,2,1,0:T(8,128)S(1)} %get-tuple-element.74), channel_id=1, source_target_pairs={{0,1},{1,2},{2,3},{3,4},{4,5},{5,6},{6,7},{7,8},{8,9},{9,10},{10,1... | collective-permute-start | bytes 196616 | tf_op jit(solution)/shard_map/ppermute | solution.py:28
  166.4 6.4 %collective-permute-start.25 = (f32[1,8,1,16,128]{4,3,2,1,0:T(8,128)S(1)}, f32[1,8,1,16,128]{4,3,2,1,0:T(8,128)S(1)}, u32[]{:S(2)}, u32[]{:S(2)}) collective-permute-start(f32[1,8,1,16,128]{4,3,2,1,0:T(8,128)S(1)} %get-tuple-element.64), channel_id=1, source_target_pairs={{0,1},{1,2},{2,3},{3,4},{4,5},{5,6},{6,7},{7,8},{8,9},{9,10},{10,1... | collective-permute-start | bytes 196616 | tf_op jit(solution)/shard_map/ppermute | solution.py:28
  182.8 6.4 %collective-permute-start.27 = (f32[1,8,1,16,128]{4,3,2,1,0:T(8,128)S(1)}, f32[1,8,1,16,128]{4,3,2,1,0:T(8,128)S(1)}, u32[]{:S(2)}, u32[]{:S(2)}) collective-permute-start(f32[1,8,1,16,128]{4,3,2,1,0:T(8,128)S(1)} %get-tuple-element.62), channel_id=1, source_target_pairs={{0,1},{1,2},{2,3},{3,4},{4,5},{5,6},{6,7},{7,8},{8,9},{9,10},{10,1... | collective-permute-start | bytes 196616 | tf_op jit(solution)/shard_map/ppermute | solution.py:28
  (10 other events, 27.5 us)
Sparse Core Ops, SparseCore 0:
  88.8 20.4 all-reduce.1
where the time goes:
time: 198 us; the launch traced here: 197 us
  waiting for transfers between devices  83.6 us (42%)
  blocking collectives  42.5 us (21%)
  starting transfers between devices  27.7 us (14%)
  between operations  15.6 us (8%)
  matrix products  12.2 us (6%)
  other arithmetic  7.88 us (4%)
  local copies, waits for them, and re-layouts  7.72 us (4%)
    ppermute x14, waiting for transfers between devices, with_halo(): lax.ppermute(lax.slice_in_dim(block, block.shape[dim] - width, None, axis...  48.3 us
    all_gather x6, blocking collectives, on_device(): piece = lax.all_gather(rates, 'node', axis=0, tiled=True)  42.5 us
    ppermute x14, starting transfers between devices, with_halo(): lax.ppermute(lax.slice_in_dim(block, 0, width, axis=dim), axis, backward)  23.6 us
    psum x1, waiting for transfers between devices, broadcast(): return lax.psum(block, axis)  20.6 us
    ppermute x14, waiting for transfers between devices, with_halo(): lax.ppermute(lax.slice_in_dim(block, 0, width, axis=dim), axis, backward)  14.7 us
    dot_general x6, matrix products, on_device(): jnp.tensordot(coefs, piece, axes=1, precision=lax.Precision.HIGHEST)  12.2 us
    ppermute x14, starting transfers between devices, with_halo(): lax.ppermute(lax.slice_in_dim(block, block.shape[dim] - width, None, axis...  4.1 us
  transfers between devices with their start and end apart: 29, of which 22 were waited for; matrix products, arithmetic and copies ran while one was open for 3% of the time, Pallas kernels for 0%

commit v1 on v0

v1 whole, which is shorter than its diff:
```python
import functools
import math

import jax
import jax.numpy as jnp
import numpy as np
from jax import lax
from jax.experimental import pallas as pl
from jax.experimental.pallas import tpu as pltpu
from jax.sharding import PartitionSpec as P

P_SIZE = 8
NODE_DEV = 1
SWEEPS = 3
JACOBI = 2
STEPS = 2
STEP_REACH = SWEEPS * JACOBI
REACH = STEPS * STEP_REACH

time_step = 0.25
cross_coef = 1.5
base_heat = 0.45
activation = 3.0

MESH = pl.DeviceIdType.MESH


def legendre_pair(count, point):
    before = 1.0
    current = point
    for degree in range(2, count + 1):
        following = ((2 * degree - 1) * point * current - (degree - 1) * before) / degree
        before = current
        current = following
    return (current, before)


def radau_value(count, point):
    high, low = legendre_pair(count, point)
    high_prev, low_prev = legendre_pair(count - 1, point)
    value = high - low
    slope_high = count * (point * high - low) / (point * point - 1.0)
    slope_low = (count - 1) * (point * high_prev - low_prev) / (point * point - 1.0)
    return (value, slope_high - slope_low)


def radau_table(count):
    roots = [1.0]
    for index in range(1, count):
        point = math.cos(2.0 * math.pi * index / (2 * count - 1))
        for repeat in range(100):
            value, slope = radau_value(count, point)
            point = point - value / slope
        roots.append(point)
    roots = sorted(roots)
    times_list = [(value + 1.0) / 2.0 for value in roots]
    times_list[-1] = 1.0
    table = []
    for row_index in range(count):
        upper = times_list[row_index]
        row_values = []
        for column in range(count):
            poly = [1.0]
            for other in range(count):
                if other != column:
                    scale = times_list[column] - times_list[other]
                    shifted = [0.0] + poly
                    scaled = [c * times_list[other] for c in poly] + [0.0]
                    poly = [(shifted[i] - scaled[i]) / scale for i in range(len(shifted))]
            integral_value = 0.0
            for power in range(len(poly)):
                integral_value += poly[power] * upper ** (power + 1) / (power + 1)
            row_values.append(integral_value)
        table.append(row_values)
    return (np.array(times_list), np.array(table))


def exchange_kernel(count, planes, hops, ids_ref, heat_ref, ext_ref, send, recv):
    me = lax.axis_index("space")
    offsets = [d for k in range(1, hops + 1) for d in (k, -k)]

    def target(offset):
        return {"space": lax.rem(me + offset + count, count)}

    barrier = pltpu.get_barrier_semaphore()
    for offset in offsets:
        pl.semaphore_signal(barrier, inc=1, device_id=target(offset), device_id_type=MESH)
    own = hops * planes
    for z in range(planes):
        for h in range(2):
            rows = pl.ds(h, 8, stride=2)
            ext_ref[own + z, 0, h] = ids_ref[z, rows, :].astype(jnp.float32)
            ext_ref[own + z, 1, h] = heat_ref[z, rows, :]
    pl.semaphore_wait(barrier, len(offsets))
    copies = []
    for index, offset in enumerate(offsets):
        copy = pltpu.make_async_remote_copy(
            src_ref=ext_ref.at[pl.ds(own, planes)],
            dst_ref=ext_ref.at[pl.ds(own - offset * planes, planes)],
            send_sem=send.at[index],
            recv_sem=recv.at[index],
            device_id=target(offset),
            device_id_type=MESH,
        )
        copy.start()
        copies.append(copy)
    for copy in copies:
        copy.wait()


def loop(low, high, body):
    def step(z, carry):
        body(z)
        return carry

    lax.fori_loop(low, high, step, 0)


def stencil(load, z, parts):
    values = {(p, h): load(p, z, h) for p in range(parts) for h in range(2)}
    doubled = {key: (v + v) * v for key, v in values.items()}
    linear = []
    for h in range(2):
        total = doubled[0, h]
        for p in range(1, parts):
            total = total + doubled[p, h]
        linear.append(1.0 - cross_coef * total)

    def at(p, h):
        v = values[p, h]
        other = values[p, 1 - h]
        rows = other + pltpu.roll(other, 1 if h == 0 else 7, 0)
        lanes = pltpu.roll(v, 1, 1) + pltpu.roll(v, v.shape[1] - 1, 1)
        planes = load(p, z - 1, h) + load(p, z + 1, h)
        return v, (rows + lanes) + planes + v * (doubled[p, h] + linear[h])

    return at


def grow_kernel(
    nodes, planes, hops, ext_ref, out_ref, start, cur, nxt, base, mob, inv, fac
):
    node_times, table = radau_table(nodes)
    node_times = [float(np.float32(t)) for t in node_times]
    table = np.asarray(np.asarray(table, np.float32), np.float64)
    mix = [
        [time_step * (table[m][j] - (node_times[m] if m == j else 0.0)) for j in range(nodes)]
        for m in range(nodes)
    ]
    own = hops * planes
    parts = P_SIZE
    mine = lax.axis_index("node")
    every = list(range(nodes))

    def fill(z):
        for h in range(2):
            ids = ext_ref[z, 0, h]
            for p in range(parts):
                start[p, z, h] = jnp.where(ids == float(p), 1.0, 0.0)

    loop(own - REACH, own + planes + REACH, fill)

    def pick(row_of, index):
        value = jnp.float32(row_of[0])
        for m in range(1, nodes):
            value = jnp.where(index == m, jnp.float32(row_of[m]), value)
        return value

    for step_index in range(STEPS):
        reach = REACH - step_index * STEP_REACH
        last_step = step_index + 1 == STEPS
        middle = 0.5 * time_step * STEPS

        def heat(z):
            for m in range(nodes):
                moment = (step_index + node_times[m]) * time_step
                bell = math.exp(-(((moment - middle) / middle) ** 2))
                for h in range(2):
                    theta = base_heat + (ext_ref[z, 1, h] - base_heat) * bell
                    rate = jnp.exp(activation * (1.0 - 1.0 / theta))
                    factor = (time_step * node_times[m]) * rate
                    inverse = 1.0 / (1.0 + 6.0 * factor)
                    mob[m, z, h] = rate
                    inv[m, z, h] = inverse
                    fac[m, z, h] = factor * inverse

        def span(body):
            loop(own - reach, own + planes + reach, body)

        reach -= 1
        span(heat)

        def first(z):
            at = stencil(lambda p, z, h: start[p, z, h], z, parts)
            for h in range(2):
                rates = [mob[j, z, h] for j in range(nodes)]
                mixes = []
                for m in range(nodes):
                    total = mix[m][0] * rates[0]
                    for j in range(1, nodes):
                        total = total + mix[m][j] * rates[j]
                    mixes.append(total * inv[m, z, h])
                for p in range(parts):
                    v, pull = at(p, h)
                    excess = pull - 6.0 * v
                    for m in range(nodes):
                        goal = inv[m, z, h] * v + mixes[m] * excess
                        base[m, p, z, h] = goal
                        nxt[m, p, z, h] = goal + fac[m, z, h] * pull

        span(first)
        a, b = nxt, cur
        for sweep_index in range(SWEEPS):
            last_sweep = sweep_index + 1 == SWEEPS
            if last_sweep:
                chosen = [mine if last_step else nodes - 1]
            else:
                chosen = every
            if sweep_index > 0:
                reach -= 1
                if last_sweep and last_step:
                    order = [lax.rem(mine + k, nodes) for k in range(nodes)]
                elif last_sweep:
                    order = [nodes - 1] + every[:-1]
                else:
                    order = every
                weights = [
                    [
                        mix[m][j]
                        if isinstance(m, int)
                        else pick([mix[q][(q + k) % nodes] for q in range(nodes)], m)
                        for k, j in enumerate(order)
                    ]
                    for m in order[: len(chosen)]
                ]

                def again(z, a=a, b=b, order=order, weights=weights):
                    ats = [
                        stencil(lambda p, z, h, m=m: a[m, p, z, h], z, parts) for m in order
                    ]
                    for h in range(2):
                        for p in range(parts):
                            pulls, flows = [], []
                            for at, j in zip(ats, order):
                                v, pull = at(p, h)
                                pulls.append(pull)
                                flows.append(mob[j, z, h] * (pull - 6.0 * v))
                            begin = start[p, z, h]
                            for k, row in enumerate(weights):
                                m = order[k]
                                goal = begin
                                for weight, flow in zip(row, flows):
                                    goal = goal + weight * flow
                                goal = goal * inv[m, z, h]
                                base[m, p, z, h] = goal
                                b[m, p, z, h] = goal + fac[m, z, h] * pulls[k]

                span(again)
                a, b = b, a
            for jacobi_index in range(1, JACOBI):
                reach -= 1
                final = last_sweep and jacobi_index + 1 == JACOBI

                def relax(z, a=a, b=b, chosen=chosen, final=final):
                    for m in chosen:
                        at = stencil(lambda p, z, h: a[m, p, z, h], z, parts)
                        for h in range(2):
                            for p in range(parts):
                                _, pull = at(p, h)
                                value = base[m, p, z, h] + fac[m, z, h] * pull
                                if not final:
                                    b[m, p, z, h] = value
                                elif last_step:
                                    out_ref[0, p, z - own, pl.ds(h, 8, stride=2), :] = value
                                else:
                                    start[p, z, h] = value

                span(relax)
                a, b = b, a


def on_device(grain_ids, peak_heat):
    count = lax.axis_size("space")
    nodes = lax.axis_size("node") * NODE_DEV
    planes, rows, lanes = grain_ids.shape
    assert rows == 16
    hops = -(-REACH // planes)
    extent = planes * (2 * hops + 1)
    half = (2, 8, lanes)
    pairs = 2 * hops
    vmem = pl.BlockSpec(memory_space=pltpu.VMEM)
    ext = pl.pallas_call(
        functools.partial(exchange_kernel, count, planes, hops),
        out_shape=jax.ShapeDtypeStruct((extent, 2) + half, jnp.float32),
        in_specs=[vmem, vmem],
        out_specs=vmem,
        scratch_shapes=[
            pltpu.SemaphoreType.DMA((pairs,)),
            pltpu.SemaphoreType.DMA((pairs,)),
        ],
        compiler_params=pltpu.CompilerParams(collective_id=0, has_side_effects=True),
    )(grain_ids, peak_heat)
    field = (nodes, P_SIZE, extent) + half
    coef = (nodes, extent) + half
    return pl.pallas_call(
        functools.partial(grow_kernel, nodes, planes, hops),
        out_shape=jax.ShapeDtypeStruct((NODE_DEV, P_SIZE, planes, rows, lanes), jnp.float32),
        in_specs=[vmem],
        out_specs=vmem,
        scratch_shapes=[pltpu.VMEM((P_SIZE, extent) + half, jnp.float32)]
        + [pltpu.VMEM(field, jnp.float32)] * 3
        + [pltpu.VMEM(coef, jnp.float32)] * 3,
        compiler_params=pltpu.CompilerParams(vmem_limit_bytes=60 * 2**20),
    )(ext)


def solution(mesh):
    in_specs = (P("space", None, None), P("space", None, None))
    out_specs = P("node", None, "space", None, None)
    return jax.shard_map(
        on_device, mesh=mesh, in_specs=in_specs, out_specs=out_specs, check_vma=False
    )
```

time: 198 us -> 41.5 us (0.21)
  waiting for transfers between devices: 83.6 us -> 0 us
  blocking collectives: 42.5 us -> 0 us
  Pallas kernels: 0 us -> 41.3 us
  starting transfers between devices: 27.7 us -> 0 us
  between operations: 15.6 us -> 0.01 us
  matrix products: 12.2 us -> 0 us
  other arithmetic: 7.88 us -> 0 us
  local copies, waits for them, and re-layouts: 7.72 us -> 0 us
    ppermute x28 -> x0, waiting for transfers between devices: 63 us -> none  [the longest x14 48.3 us: with_halo(): lax.ppermute(lax.slice_in_dim(block, block.shape[dim] - width, None, axis...]
    all_gather x6 -> x0, blocking collectives: 42.5 us -> none  [on_device(): piece = lax.all_gather(rates, 'node', axis=0, tiled=True)]
    pallas_call x0 -> x2, Pallas kernels: none -> 41.3 us  [the longest x1 27.9 us: on_device(): pl.pallas_call(functools.partial(grow_kernel, nodes, planes, hops), out_s...]
    ppermute x28 -> x0, starting transfers between devices: 27.7 us -> none  [the longest x14 23.6 us: with_halo(): lax.ppermute(lax.slice_in_dim(block, 0, width, axis=dim), axis, backward)]
    psum x1 -> x0, waiting for transfers between devices: 20.6 us -> none  [broadcast(): return lax.psum(block, axis)]
    dot_general x6 -> x0, matrix products: 12.2 us -> none  [on_device(): jnp.tensordot(coefs, piece, axes=1, precision=lax.Precision.HIGHEST)]
    slice x70 -> x0, local copies, waits for them, and re-layouts: 6.61 us -> none  [the longest x28 3.7 us: near_sum(): return result + jnp.roll(inner, -1, -1) + jnp.roll(inner, 1, -1)]
    reduce_sum x14 -> x0, other arithmetic: 3.06 us -> none  [drive(): total = jnp.sum(squares, axis=-4, keepdims=True)]
  transfers between devices with their start and end apart: 29 -> 0, of which waited for: 22 -> 0; matrix products, arithmetic and copies ran while one was open for 3% -> 0% of each run, Pallas kernels for 0% -> 0%
where the time goes in v1:
time: 41.5 us; the launch traced here: 41.3 us
  Pallas kernels  41.3 us (100%)
    pallas_call x1, Pallas kernels, on_device(): pl.pallas_call(functools.partial(grow_kernel, nodes, planes, hops), out_s...  27.9 us
    pallas_call x1, Pallas kernels, on_device(): pl.pallas_call(functools.partial(exchange_kernel, count, planes, hops), o...  13.4 us

profile of v1, /device:TPU:0, one launch (start us, length us, event | category | flops | bytes accessed | tf_op | source)
XLA Modules:
  0.0 41.3 jit_solution(7845446641048067396)
XLA Ops:
  0.0 13.4 %shard_map.28.ext_ref = f32[28,2,2,8,128]{4,3,2,1,0:T(8,128)} custom-call(s32[4,16,128]{2,1,0:T(8,128)} %ids_ref.1, f32[4,16,128]{2,1,0:T(8,128)} %heat_ref.1), custom_call_target="tpu_custom_call" | custom-call | tf_op jit(solution)/shard_map/pallas_call | solution.py:292
  13.4 27.9 %shard_map.29 = f32[1,8,4,16,128]{4,3,2,1,0:T(8,128)} custom-call(f32[28,2,2,8,128]{4,3,2,1,0:T(8,128)} %shard_map.28.ext_ref), custom_call_target="tpu_custom_call" | custom-call | tf_op jit(solution)/shard_map/pallas_call | solution.py:305

commit v2 on v1

--- a/solution.py
+++ b/solution.py
@@ -108,12 +108,17 @@
         copy.wait()
 
 
-def loop(low, high, body):
-    def step(z, carry):
+def loop(low, high, body, unroll=1):
+    rounds = (high - low) // unroll
+
+    def step(index, carry):
+        for k in range(unroll):
+            body(low + index * unroll + k)
+        return carry
+
+    lax.fori_loop(0, rounds, step, 0)
+    for z in range(low + rounds * unroll, high):
         body(z)
-        return carry
-
-    lax.fori_loop(low, high, step, 0)
 
 
 def stencil(load, z, parts):
@@ -121,10 +126,10 @@
     doubled = {key: (v + v) * v for key, v in values.items()}
     linear = []
     for h in range(2):
-        total = doubled[0, h]
-        for p in range(1, parts):
-            total = total + doubled[p, h]
-        linear.append(1.0 - cross_coef * total)
+        terms = [doubled[p, h] for p in range(parts)]
+        while len(terms) > 1:
+            terms = [sum(terms[i + 1 : i + 2], terms[i]) for i in range(0, len(terms), 2)]
+        linear.append(1.0 - cross_coef * terms[0])
 
     def at(p, h):
         v = values[p, h]
@@ -185,7 +190,7 @@
                     fac[m, z, h] = factor * inverse
 
         def span(body):
-            loop(own - reach, own + planes + reach, body)
+            loop(own - reach, own + planes + reach, body, 4 if nodes <= 2 else 1)
 
         reach -= 1
         span(heat)

time: 41.5 us -> 30.8 us (0.74)
  Pallas kernels: 41.3 us -> 30.6 us
    pallas_call x1, Pallas kernels: 27.9 us -> 17.2 us  [on_device(): pl.pallas_call(functools.partial(grow_kernel, nodes, planes, hops), out_s...]
where the time goes in v2:
time: 30.8 us; the launch traced here: 30.6 us
  Pallas kernels  30.6 us (99%)
    pallas_call x1, Pallas kernels, on_device(): pl.pallas_call(functools.partial(grow_kernel, nodes, planes, hops), out_s...  17.2 us
    pallas_call x1, Pallas kernels, on_device(): pl.pallas_call(functools.partial(exchange_kernel, count, planes, hops), o...  13.4 us

profile of v2, /device:TPU:0, one launch (start us, length us, event | category | flops | bytes accessed | tf_op | source)
XLA Modules:
  0.0 30.6 jit_solution(8985953624813399923)
XLA Ops:
  0.0 13.4 %shard_map.28.ext_ref = f32[28,2,2,8,128]{4,3,2,1,0:T(8,128)} custom-call(s32[4,16,128]{2,1,0:T(8,128)} %ids_ref.1, f32[4,16,128]{2,1,0:T(8,128)} %heat_ref.1), custom_call_target="tpu_custom_call" | custom-call | tf_op jit(solution)/shard_map/pallas_call | solution.py:297
  13.4 17.2 %shard_map.29 = f32[1,8,4,16,128]{4,3,2,1,0:T(8,128)} custom-call(f32[28,2,2,8,128]{4,3,2,1,0:T(8,128)} %shard_map.28.ext_ref), custom_call_target="tpu_custom_call" | custom-call | tf_op jit(solution)/shard_map/pallas_call | solution.py:310

commit v3 on v2

v3 whole, which is shorter than its diff:
```python
import functools
import math

import jax
import jax.numpy as jnp
import numpy as np
from jax import lax
from jax.experimental import pallas as pl
from jax.experimental.pallas import tpu as pltpu
from jax.sharding import PartitionSpec as P

P_SIZE = 8
NODE_DEV = 1
SWEEPS = 3
JACOBI = 2
STEPS = 2
STEP_REACH = SWEEPS * JACOBI
REACH = STEPS * STEP_REACH

time_step = 0.25
cross_coef = 1.5
base_heat = 0.45
activation = 3.0

MESH = pl.DeviceIdType.MESH


def legendre_pair(count, point):
    before = 1.0
    current = point
    for degree in range(2, count + 1):
        following = ((2 * degree - 1) * point * current - (degree - 1) * before) / degree
        before = current
        current = following
    return (current, before)


def radau_value(count, point):
    high, low = legendre_pair(count, point)
    high_prev, low_prev = legendre_pair(count - 1, point)
    value = high - low
    slope_high = count * (point * high - low) / (point * point - 1.0)
    slope_low = (count - 1) * (point * high_prev - low_prev) / (point * point - 1.0)
    return (value, slope_high - slope_low)


def radau_table(count):
    roots = [1.0]
    for index in range(1, count):
        point = math.cos(2.0 * math.pi * index / (2 * count - 1))
        for repeat in range(100):
            value, slope = radau_value(count, point)
            point = point - value / slope
        roots.append(point)
    roots = sorted(roots)
    times_list = [(value + 1.0) / 2.0 for value in roots]
    times_list[-1] = 1.0
    table = []
    for row_index in range(count):
        upper = times_list[row_index]
        row_values = []
        for column in range(count):
            poly = [1.0]
            for other in range(count):
                if other != column:
                    scale = times_list[column] - times_list[other]
                    shifted = [0.0] + poly
                    scaled = [c * times_list[other] for c in poly] + [0.0]
                    poly = [(shifted[i] - scaled[i]) / scale for i in range(len(shifted))]
            integral_value = 0.0
            for power in range(len(poly)):
                integral_value += poly[power] * upper ** (power + 1) / (power + 1)
            row_values.append(integral_value)
        table.append(row_values)
    return (np.array(times_list), np.array(table))


def loop(low, high, body, unroll=1):
    rounds = (high - low) // unroll

    def step(index, carry):
        for k in range(unroll):
            body(low + index * unroll + k)
        return carry

    lax.fori_loop(0, rounds, step, 0)
    for z in range(low + rounds * unroll, high):
        body(z)


def stencil(load, z, parts):
    values = {(p, h): load(p, z, h) for p in range(parts) for h in range(2)}
    doubled = {key: (v + v) * v for key, v in values.items()}
    linear = []
    for h in range(2):
        terms = [doubled[p, h] for p in range(parts)]
        while len(terms) > 1:
            terms = [sum(terms[i + 1 : i + 2], terms[i]) for i in range(0, len(terms), 2)]
        linear.append(1.0 - cross_coef * terms[0])

    def at(p, h):
        v = values[p, h]
        other = values[p, 1 - h]
        rows = other + pltpu.roll(other, 1 if h == 0 else 7, 0)
        lanes = pltpu.roll(v, 1, 1) + pltpu.roll(v, v.shape[1] - 1, 1)
        planes = load(p, z - 1, h) + load(p, z + 1, h)
        return v, (rows + lanes) + planes + v * (doubled[p, h] + linear[h])

    return at


def grow_kernel(
    count, nodes, planes, hops, skew, ids_ref, heat_ref, out_ref,
    ext_ref, starts, stages, bases, mob, inv, fac, send, recv,
):
    node_times, table = radau_table(nodes)
    node_times = [float(np.float32(t)) for t in node_times]
    table = np.asarray(np.asarray(table, np.float32), np.float64)
    mix = [
        [time_step * (table[m][j] - (node_times[m] if m == j else 0.0)) for j in range(nodes)]
        for m in range(nodes)
    ]
    own = hops * planes
    parts = P_SIZE
    me = lax.axis_index("space")
    mine = lax.axis_index("node")
    every = list(range(nodes))
    unroll = 4 if skew else 1

    offsets = [d for k in range(1, hops + 1) for d in (k, -k)]

    def target(offset):
        return {"space": lax.rem(me + offset + count, count)}

    barrier = pltpu.get_barrier_semaphore()
    for offset in offsets:
        pl.semaphore_signal(barrier, inc=1, device_id=target(offset), device_id_type=MESH)
    for z in range(planes):
        for h in range(2):
            rows = pl.ds(h, 8, stride=2)
            ext_ref[own + z, 0, h] = ids_ref[z, rows, :].astype(jnp.float32)
            ext_ref[own + z, 1, h] = heat_ref[z, rows, :]
    pl.semaphore_wait(barrier, len(offsets))
    copies = []
    for index, offset in enumerate(offsets):
        copy = pltpu.make_async_remote_copy(
            src_ref=ext_ref.at[pl.ds(own, planes)],
            dst_ref=ext_ref.at[pl.ds(own - offset * planes, planes)],
            send_sem=send.at[index],
            recv_sem=recv.at[index],
            device_id=target(offset),
            device_id_type=MESH,
        )
        copy.start()
        copies.append(copy)

    def fill(z):
        for h in range(2):
            ids = ext_ref[z, 0, h]
            for p in range(parts):
                starts[0, p, z, h] = jnp.where(ids == float(p), 1.0, 0.0)

    def pick(row_of, index):
        value = jnp.float32(row_of[0])
        for m in range(1, nodes):
            value = jnp.where(index == m, jnp.float32(row_of[m]), value)
        return value

    def heat(step_index, z):
        middle = 0.5 * time_step * STEPS
        for m in range(nodes):
            moment = (step_index + node_times[m]) * time_step
            bell = math.exp(-(((moment - middle) / middle) ** 2))
            for h in range(2):
                theta = base_heat + (ext_ref[z, 1, h] - base_heat) * bell
                rate = jnp.exp(activation * (1.0 - 1.0 / theta))
                factor = (time_step * node_times[m]) * rate
                inverse = 1.0 / (1.0 + 6.0 * factor)
                mob[m, z, h] = rate
                inv[m, z, h] = inverse
                fac[m, z, h] = factor * inverse

    def prepare(z):
        fill(z)
        heat(0, z)

    def level(step_index, number):
        last_step = step_index + 1 == STEPS
        sweep_index, jacobi_index = divmod(number, JACOBI)
        last_sweep = sweep_index + 1 == SWEEPS
        start = starts.at[step_index % starts.shape[0]]
        following = starts.at[(step_index + 1) % starts.shape[0]]
        base = bases.at[sweep_index % bases.shape[0]]
        a = stages.at[(number - 1) % stages.shape[0]]
        b = stages.at[number % stages.shape[0]]

        def first(z):
            at = stencil(lambda p, z, h: start[p, z, h], z, parts)
            for h in range(2):
                rates = [mob[j, z, h] for j in range(nodes)]
                mixes = []
                for m in range(nodes):
                    total = mix[m][0] * rates[0]
                    for j in range(1, nodes):
                        total = total + mix[m][j] * rates[j]
                    mixes.append(total * inv[m, z, h])
                for p in range(parts):
                    v, pull = at(p, h)
                    excess = pull - 6.0 * v
                    for m in range(nodes):
                        goal = inv[m, z, h] * v + mixes[m] * excess
                        base[m, p, z, h] = goal
                        b[m, p, z, h] = goal + fac[m, z, h] * pull

        if not last_sweep:
            order, chosen = every, every
        elif last_step:
            order = [lax.rem(mine + k, nodes) for k in range(nodes)]
            chosen = order[:1]
        else:
            order = [nodes - 1] + every[:-1]
            chosen = order[:1]
        weights = [
            [
                mix[m][j]
                if isinstance(m, int)
                else pick([mix[q][(q + k) % nodes] for q in range(nodes)], m)
                for k, j in enumerate(order)
            ]
            for m in chosen
        ]

        def again(z):
            ats = [stencil(lambda p, z, h, m=m: a[m, p, z, h], z, parts) for m in order]
            for h in range(2):
                for p in range(parts):
                    pulls, flows = [], []
                    for at, j in zip(ats, order):
                        v, pull = at(p, h)
                        pulls.append(pull)
                        flows.append(mob[j, z, h] * (pull - 6.0 * v))
                    begin = start[p, z, h]
                    for k, row in enumerate(weights):
                        m = order[k]
                        goal = begin
                        for weight, flow in zip(row, flows):
                            goal = goal + weight * flow
                        goal = goal * inv[m, z, h]
                        base[m, p, z, h] = goal
                        b[m, p, z, h] = goal + fac[m, z, h] * pulls[k]

        final = number + 1 == STEP_REACH

        def relax(z):
            for m in chosen:
                at = stencil(lambda p, z, h: a[m, p, z, h], z, parts)
                for h in range(2):
                    for p in range(parts):
                        _, pull = at(p, h)
                        value = base[m, p, z, h] + fac[m, z, h] * pull
                        if not final:
                            b[m, p, z, h] = value
                        elif last_step:
                            out_ref[0, p, z - own, pl.ds(h, 8, stride=2), :] = value
                        else:
                            following[p, z, h] = value

        if jacobi_index > 0:
            return relax
        return again if sweep_index > 0 else first

    done = 0
    if skew:
        loop(own, own + planes, prepare, 2)
        copies[0].wait_recv()
        copies[1].wait_recv()
        loop(own - planes, own, prepare, 2)
        loop(own + planes, own + 2 * planes, prepare, 2)
        for number in range(STEP_REACH):
            reach = planes - 1 - number
            if planes + 2 * reach > 0:
                loop(own - reach, own + planes + reach, level(0, number), 2)

        def ring(turn, carry):
            distance = (2 + turn // 2) * planes
            side = lax.rem(turn, 2)
            pltpu.make_async_remote_copy(
                src_ref=ext_ref.at[pl.ds(own, planes)],
                dst_ref=ext_ref.at[pl.ds(own, planes)],
                send_sem=send.at[2 + turn],
                recv_sem=recv.at[2 + turn],
                device_id=target(1),
                device_id_type=MESH,
            ).wait_recv()
            low = own + jnp.where(side == 0, -distance, distance)
            inward = jnp.where(side == 0, 1, -1)
            for k in range(planes):
                prepare(low + k)
            for number in range(STEP_REACH):
                body = level(0, number)
                for k in range(planes):
                    body(low + inward * (number + 1) + k)
            return carry

        lax.fori_loop(0, 2 * (hops - 1), ring, 0)
        done = 1
    else:
        for copy in copies:
            copy.wait_recv()
        loop(own - REACH, own + planes + REACH, fill)
    for step_index in range(done, STEPS):
        reach = REACH - step_index * STEP_REACH - 1
        loop(own - reach, own + planes + reach, functools.partial(heat, step_index), unroll)
        for number in range(STEP_REACH):
            body = level(step_index, number)
            loop(own - reach + number, own + planes + reach - number, body, unroll)
    for copy in copies:
        copy.wait_send()


def on_device(grain_ids, peak_heat):
    count = lax.axis_size("space")
    nodes = lax.axis_size("node") * NODE_DEV
    planes, rows, lanes = grain_ids.shape
    assert rows == 16
    hops = -(-REACH // planes)
    extent = planes * (2 * hops + 1)
    skew = nodes <= 2 and hops * planes == REACH and planes + 2 * (planes - STEP_REACH) >= 0
    half = (2, 8, lanes)
    pairs = 2 * hops
    vmem = pl.BlockSpec(memory_space=pltpu.VMEM)
    field = (nodes, P_SIZE, extent) + half
    coef = (nodes, extent) + half
    return pl.pallas_call(
        functools.partial(grow_kernel, count, nodes, planes, hops, skew),
        out_shape=jax.ShapeDtypeStruct((NODE_DEV, P_SIZE, planes, rows, lanes), jnp.float32),
        in_specs=[vmem, vmem],
        out_specs=vmem,
        scratch_shapes=[
            pltpu.VMEM((extent, 2) + half, jnp.float32),
            pltpu.VMEM((2 if skew else 1, P_SIZE, extent) + half, jnp.float32),
            pltpu.VMEM(((STEP_REACH - 1 if skew else 2),) + field, jnp.float32),
            pltpu.VMEM(((SWEEPS if skew else 1),) + field, jnp.float32),
        ]
        + [pltpu.VMEM(coef, jnp.float32)] * 3
        + [pltpu.SemaphoreType.DMA((pairs,))] * 2,
        compiler_params=pltpu.CompilerParams(
            collective_id=0, has_side_effects=True, vmem_limit_bytes=60 * 2**20
        ),
    )(grain_ids, peak_heat)


def solution(mesh):
    in_specs = (P("space", None, None), P("space", None, None))
    out_specs = P("node", None, "space", None, None)
    return jax.shard_map(
        on_device, mesh=mesh, in_specs=in_specs, out_specs=out_specs, check_vma=False
    )
```

time: 30.8 us -> 29.8 us (0.968)
  the two profiles are of different devices: /device:TPU:0 before, /device:TPU:1 now
where the time goes in v3:
time: 29.8 us; the launch traced here: 29.6 us
  Pallas kernels  27.9 us (94%)
  local copies, waits for them, and re-layouts  1.67 us (6%)
    pallas_call x1, Pallas kernels, on_device(): pl.pallas_call(functools.partial(grow_kernel, count, nodes, planes, hops,...  27.9 us
    unnamed x1, local copies, waits for them, and re-layouts  1.67 us

profile of v3, /device:TPU:1, one launch (start us, length us, event | category | flops | bytes accessed | tf_op | source)
XLA Modules:
  0.0 29.6 jit_solution(16166054788905573785)
XLA Ops:
  0.0 27.9 %shard_map.28 = f32[1,8,4,16,128]{4,3,2,1,0:T(8,128)} custom-call(s32[4,16,128]{2,1,0:T(8,128)} %ids_ref.1, f32[4,16,128]{2,1,0:T(8,128)} %heat_ref.1), custom_call_target="tpu_custom_call" | custom-call | tf_op jit(solution)/shard_map/pallas_call | solution.py:334
  27.9 1.7 %copy.4 = f32[1,8,4,16,128]{4,3,2,1,0:T(8,128)} copy(f32[1,8,4,16,128]{4,3,2,1,0:T(8,128)} %shard_map.28) | data formatting | bytes 524288
